TPU v7x, 512 devices: a whole 4x8x8 slice. The times are simulated.
512 devices in a mesh: depth: 8 (over y), tile: 64 (over z, x, core).
Axes of the slice: x: 4, y: 8, z: 8, core: 2. Of those that a mesh axis runs over, the one named last changes fastest.
Arguments:
- labels: int32 [64, 1024, 1024], P('depth', 'tile'), may hold values from 0 to 255
- depth_order: int32 [64, 8], P('tile'), may hold values from 0 to 7, each once within a row
- opacity_table: int32 [256], replicated, may hold values from 0 to 255
- colour_map: int32 [3, 256], replicated, may hold values from 0 to 255
Outputs:
- frame: float32 [4, 64, 16, 1024], P(None, 'tile', 'depth')
Inputs may be any that keep to these rules, and one draw needn't show every extreme that they name: `depth_order`: each row names every rank once.
All inputs are finite; a program needn't handle non-finite values.
Results may differ from a plain program's by a relative error of at most 0.0003.
Values sent between devices are 32-bit elements; how exact they have to be, the bound alone decides.
A program may use at most 64 MiB of HBM per device.

v0:
```python
import math

import jax
import jax.numpy as jnp
from jax import lax
from jax.sharding import PartitionSpec as P

LIGHT_Z = 0.8
LIGHT_Y = 0.36
LIGHT_X = 0.48
KEY_VALUE = 0.18


def padded_2(shard, sides, width):
    for axis, dim in sides:
        size, length = (lax.axis_size(axis), shard.shape[dim])
        up = [(i, (i + 1) % size) for i in range(size - 1)]
        down = [(j, i) for i, j in up]
        last = lax.slice_in_dim(shard, length - width, length, axis=dim)
        initial = lax.slice_in_dim(shard, 0, width, axis=dim)
        before = lax.ppermute(last, axis, up)
        after = lax.ppermute(initial, axis, down)
        shard = jnp.concatenate([before, shard, after], axis=dim)
    return shard


def lookup(labels, levels):
    cells = labels.size
    width = math.gcd(cells, 16384)
    blocks = labels.reshape(cells // width, width)
    values = jnp.arange(levels.shape[1], dtype=jnp.int32)

    def one_block(piece):
        onehot = (piece[None, :] == values[:, None]).astype(jnp.bfloat16)
        return jnp.dot(levels, onehot, preferred_element_type=jnp.float32)

    found = lax.map(one_block, blocks)
    return jnp.moveaxis(found, 1, 0).reshape((levels.shape[0],) + labels.shape)


def shading(padded):
    grad_z = 0.5 * (padded[2:, 1:-1, 1:-1] - padded[:-2, 1:-1, 1:-1])
    grad_y = 0.5 * (padded[1:-1, 2:, 1:-1] - padded[1:-1, :-2, 1:-1])
    grad_x = 0.5 * (padded[1:-1, 1:-1, 2:] - padded[1:-1, 1:-1, :-2])
    length = jnp.sqrt(grad_z * grad_z + grad_y * grad_y + grad_x * grad_x)
    facing = jnp.abs(grad_z * LIGHT_Z + grad_y * LIGHT_Y + grad_x * LIGHT_X) / jnp.maximum(
        length, 0.25
    )
    return 0.3 + 0.7 * facing


def combine(colours, passes, ranks):
    before = ranks[None, :] < ranks[:, None]
    factors = jnp.where(before[:, :, None, None], passes[None], jnp.float32(1.0))
    ahead = jnp.prod(factors, axis=1)
    return (jnp.sum(ahead[None] * colours, axis=1), jnp.prod(passes, axis=0))


def body(labels, depth_order, opacity_table, colour_map):
    groups = lax.axis_size("depth")
    strips = lax.axis_size("tile")
    depth_size, row_count, col_count = labels.shape
    depth_total = depth_size * groups
    row_total = row_count * strips
    piece_rows = row_count // groups
    levels = jnp.concatenate([opacity_table[None, :], colour_map], axis=0).astype(jnp.bfloat16)
    found = lookup(labels, levels) / 255.0
    density = found[0]
    colour = found[1:]
    padded = padded_2(density, (("depth", 0), ("tile", 1)), 1)
    padded = jnp.pad(padded, ((0, 0), (0, 0), (1, 1)))
    shade = shading(padded)
    first_row = lax.axis_index("tile") * row_count
    ramp = (
        0.5
        + ((first_row + jnp.arange(row_count, dtype=jnp.int32)).astype(jnp.float32) + 0.5)
        / row_total
    )
    passing = jnp.exp(-2.0 * density / depth_total)
    weight = (1.0 - passing) * shade * ramp[None, :, None]
    samples = colour * weight[None]
    through = jnp.cumprod(passing, axis=0)
    ahead_in = jnp.concatenate([jnp.ones_like(through[:1]), through[:-1]], axis=0)
    brick_colour = jnp.sum(ahead_in[None] * samples, axis=1)
    brick_pass = through[-1]
    ranks = depth_order[0]
    stacked = jnp.concatenate([brick_colour, brick_pass[None]], axis=0).reshape(
        4, groups, piece_rows, col_count
    )
    arrived = lax.all_to_all(stacked, "depth", split_axis=1, concat_axis=1, tiled=True)
    composite, total_pass = combine(arrived[:3], arrived[3], ranks)
    lum = 0.2126 * composite[0] + 0.7152 * composite[1] + 0.0722 * composite[2]
    log_sum = lax.psum(jnp.sum(jnp.log(0.05 + lum)), ("depth", "tile"))
    scale = KEY_VALUE / jnp.exp(log_sum / (row_total * col_count))
    mapped = composite * scale / (1.0 + composite * scale)
    frame = jnp.concatenate([mapped, (1.0 - total_pass)[None]], axis=0)
    return frame[:, None]


def solution(mesh):
    in_specs = (P("depth", "tile", None), P("tile", None), P(), P())
    out_specs = P(None, "tile", "depth", None)
    return jax.shard_map(body, mesh=mesh, in_specs=in_specs, out_specs=out_specs, check_vma=False)
```

profile of v0, /device:TPU:1, one launch (start us, length us, event | category | flops | bytes accessed | tf_op | source)
XLA Modules:
  0.0 185.7 jit_solution(4307051076269908540)
XLA Ops:
  0.0 1.3 copy.34
  1.4 0.7 convert.8
  2.0 0.7 convert.7
  2.7 26.5 %while.11 = (s32[]{:T(128)}, f32[8,4,16384]{2,1,0:T(4,128)}, s32[8,16384]{1,0:T(8,128)S(1)}, bf16[4,256]{1,0:T(4,128)(2,1)S(1)}, s32[]{:T(128)}) while((s32[]{:T(128)}, f32[8,4,16384]{2,1,0:T(4,128)}, s32[8,16384]{1,0:T(8,128)S(1)}, bf16[4,256]{1,0:T(4,128)(2,1)S(1)}, s32[]{:T(128)}) %tuple.27), condition=%wide.region_1.2_spmd.clone, body=%wide.region_0.1_spmd.clone.sunk | while | flops 37748736 | bytes 461377 | solution.py:37
  2.8 3.2 %fusion.23 = f32[8,4,16384]{2,1,0:T(4,128)} fusion(f32[8,4,16384]{2,1,0:T(4,128)} %get-tuple-element.88, s32[]{:T(128)} %get-tuple-element.87, bf16[4,256]{1,0:T(4,128)(2,1)S(1)} %get-tuple-element.95, s32[16384]{0:T(1024)S(1)} %bitcast.51), kind=kOutput, calls=%fused_computation.2.clone.1 | convolution fusion | flops 37748736 | bytes 330240 | tf_op jit(solution)/shard_map/while/body/eval_jaxpr/dot_general | solution.py:35
  6.1 3.3 %fusion.23 = f32[8,4,16384]{2,1,0:T(4,128)} fusion(f32[8,4,16384]{2,1,0:T(4,128)} %get-tuple-element.88, s32[]{:T(128)} %get-tuple-element.87, bf16[4,256]{1,0:T(4,128)(2,1)S(1)} %get-tuple-element.95, s32[16384]{0:T(1024)S(1)} %bitcast.51), kind=kOutput, calls=%fused_computation.2.clone.1 | convolution fusion | flops 37748736 | bytes 330240 | tf_op jit(solution)/shard_map/while/body/eval_jaxpr/dot_general | solution.py:35
  9.4 3.3 %fusion.23 = f32[8,4,16384]{2,1,0:T(4,128)} fusion(f32[8,4,16384]{2,1,0:T(4,128)} %get-tuple-element.88, s32[]{:T(128)} %get-tuple-element.87, bf16[4,256]{1,0:T(4,128)(2,1)S(1)} %get-tuple-element.95, s32[16384]{0:T(1024)S(1)} %bitcast.51), kind=kOutput, calls=%fused_computation.2.clone.1 | convolution fusion | flops 37748736 | bytes 330240 | tf_op jit(solution)/shard_map/while/body/eval_jaxpr/dot_general | solution.py:35
  12.7 3.3 %fusion.23 = f32[8,4,16384]{2,1,0:T(4,128)} fusion(f32[8,4,16384]{2,1,0:T(4,128)} %get-tuple-element.88, s32[]{:T(128)} %get-tuple-element.87, bf16[4,256]{1,0:T(4,128)(2,1)S(1)} %get-tuple-element.95, s32[16384]{0:T(1024)S(1)} %bitcast.51), kind=kOutput, calls=%fused_computation.2.clone.1 | convolution fusion | flops 37748736 | bytes 330240 | tf_op jit(solution)/shard_map/while/body/eval_jaxpr/dot_general | solution.py:35
  16.0 3.3 %fusion.23 = f32[8,4,16384]{2,1,0:T(4,128)} fusion(f32[8,4,16384]{2,1,0:T(4,128)} %get-tuple-element.88, s32[]{:T(128)} %get-tuple-element.87, bf16[4,256]{1,0:T(4,128)(2,1)S(1)} %get-tuple-element.95, s32[16384]{0:T(1024)S(1)} %bitcast.51), kind=kOutput, calls=%fused_computation.2.clone.1 | convolution fusion | flops 37748736 | bytes 330240 | tf_op jit(solution)/shard_map/while/body/eval_jaxpr/dot_general | solution.py:35
  19.4 3.3 %fusion.23 = f32[8,4,16384]{2,1,0:T(4,128)} fusion(f32[8,4,16384]{2,1,0:T(4,128)} %get-tuple-element.88, s32[]{:T(128)} %get-tuple-element.87, bf16[4,256]{1,0:T(4,128)(2,1)S(1)} %get-tuple-element.95, s32[16384]{0:T(1024)S(1)} %bitcast.51), kind=kOutput, calls=%fused_computation.2.clone.1 | convolution fusion | flops 37748736 | bytes 330240 | tf_op jit(solution)/shard_map/while/body/eval_jaxpr/dot_general | solution.py:35
  22.7 3.3 %fusion.23 = f32[8,4,16384]{2,1,0:T(4,128)} fusion(f32[8,4,16384]{2,1,0:T(4,128)} %get-tuple-element.88, s32[]{:T(128)} %get-tuple-element.87, bf16[4,256]{1,0:T(4,128)(2,1)S(1)} %get-tuple-element.95, s32[16384]{0:T(1024)S(1)} %bitcast.51), kind=kOutput, calls=%fused_computation.2.clone.1 | convolution fusion | flops 37748736 | bytes 330240 | tf_op jit(solution)/shard_map/while/body/eval_jaxpr/dot_general | solution.py:35
  26.0 3.3 %fusion.23 = f32[8,4,16384]{2,1,0:T(4,128)} fusion(f32[8,4,16384]{2,1,0:T(4,128)} %get-tuple-element.88, s32[]{:T(128)} %get-tuple-element.87, bf16[4,256]{1,0:T(4,128)(2,1)S(1)} %get-tuple-element.95, s32[16384]{0:T(1024)S(1)} %bitcast.51), kind=kOutput, calls=%fused_computation.2.clone.1 | convolution fusion | flops 37748736 | bytes 330240 | tf_op jit(solution)/shard_map/while/body/eval_jaxpr/dot_general | solution.py:35
  29.3 2.1 %multiply_bitcast_fusion = f32[4,8,16384]{2,0,1:T(4,128)S(1)} fusion(f32[8,4,16384]{2,1,0:T(4,128)} %get-tuple-element.32), kind=kLoop, calls=%fused_computation.6 | loop fusion | flops 524288 | bytes 4194304 | tf_op jit(solution)/shard_map/div | solution.py:67
  31.4 2.5 %reshape.81 = f32[4,8,16,1024]{3,2,0,1:T(8,128)} reshape(f32[4,8,16384]{2,0,1:T(4,128)S(1)} %multiply_bitcast_fusion) | data formatting | bytes 4194304 | tf_op jit(solution)/shard_map/div | solution.py:67
  33.9 0.9 slice_bitcast_fusion.1
  34.8 4.0 %collective-permute-start.1 = (f32[1,16,1024]{2,1,0:T(8,128)S(1)}, f32[1,16,1024]{2,1,0:T(8,128)S(1)}, u32[]{:S(2)}, u32[]{:S(2)}) collective-permute-start(f32[1,16,1024]{2,1,0:T(8,128)S(1)} %get-tuple-element.52), channel_id=1, source_target_pairs={{0,64},{64,128},{128,192},{192,256},{256,320},{320,384},{384,448},... | collective-permute-start | bytes 196616 | tf_op jit(solution)/shard_map/ppermute | solution.py:21
  38.9 1.3 collective-permute-start
  40.2 1.3 slice_reduce_fusion
  41.5 1.1 fusion.9
  42.7 0.0 collective-permute-done.1
  42.7 0.3 constant_dynamic-update-slice_fusion.1
  43.0 0.9 collective-permute-done
  43.9 0.7 fusion.18
  44.6 7.2 %collective-permute-start.2 = (f32[10,1,1024]{2,1,0:T(1,128)}, f32[10,1,1024]{2,1,0:T(1,128)S(1)}, u32[]{:S(2)}, u32[]{:S(2)}) collective-permute-start(f32[10,1,1024]{2,1,0:T(1,128)} %get-tuple-element.54), channel_id=1, source_target_pairs={{1,0},{2,1},{3,2},{4,3},{5,4},{6,5},{7,6},{8,7},{9,8},{10,9},{11,1... | collective-permute-start | bytes 122888 | tf_op jit(solution)/shard_map/ppermute | solution.py:22
  51.7 1.9 %collective-permute-start.3 = (f32[10,1,1024]{2,1,0:T(1,128)S(1)}, f32[10,1,1024]{2,1,0:T(1,128)S(1)}, u32[]{:S(2)}, u32[]{:S(2)}) collective-permute-start(f32[10,1,1024]{2,1,0:T(1,128)S(1)} %get-tuple-element.53), channel_id=1, source_target_pairs={{0,1},{1,2},{2,3},{3,4},{4,5},{5,6},{6,7},{7,8},{8,9},{9,10},{10,1... | collective-permute-start | bytes 122888 | tf_op jit(solution)/shard_map/ppermute | solution.py:21
  53.7 1.1 copy.47
  54.8 1.9 %slice.103 = f32[3,8,16384]{2,0,1:T(4,128)} slice(f32[4,8,16384]{2,0,1:T(4,128)S(1)} %multiply_bitcast_fusion), slice={[1:4], [0:8], [0:16384]} | slice | bytes 3145728 | tf_op jit(solution)/shard_map/slice | solution.py:69
  56.7 0.0 slice-start
  56.7 3.0 %reshape.80 = f32[3,8,16,1024]{3,2,0,1:T(8,128)S(1)} reshape(f32[3,8,16384]{2,0,1:T(4,128)} %slice.103) | data formatting | bytes 3145728 | tf_op jit(solution)/shard_map/slice | solution.py:69
  59.7 0.0 slice-done
  59.7 0.0 copy-start
  59.8 0.0 collective-permute-done.2
  59.8 0.0 collective-permute-done.3
  59.8 0.6 select_maximum_fusion
  60.4 0.4 copy-done
  60.8 0.8 multiply_multiply_fusion
  61.6 0.0 slice-start.1
  61.6 0.3 fusion.5
  61.9 0.5 slice-done.1
  62.4 0.0 copy-start.1
  62.5 0.2 copy.27
  62.6 0.9 copy.28
  63.5 5.0 %all-to-all-start = ((f32[4,8,2,1024]{3,2,0,1:T(2,128)}), f32[4,8,2,1024]{3,2,0,1:T(2,128)S(1)}, u32[]{:S(2)}, u32[]{:S(2)}) async-start(f32[4,8,2,1024]{3,2,0,1:T(2,128)} %copy.28), calls=%async_computation | async-start | bytes 524288 | tf_op jit(solution)/shard_map/all_to_all | solution.py:90
  68.5 0.0 copy-done.1
  68.5 0.1 broadcast_compare_fusion
  68.6 12.3 %all-to-all-done = f32[4,8,2,1024]{3,2,0,1:T(2,128)S(1)} async-done(((f32[4,8,2,1024]{3,2,0,1:T(2,128)}), f32[4,8,2,1024]{3,2,0,1:T(2,128)S(1)}, u32[]{:S(2)}, u32[]{:S(2)}) %all-to-all-start) | async-done | bytes 262176 | tf_op jit(solution)/shard_map/all_to_all | solution.py:90
  81.0 0.2 select_reduce_fusion
  81.3 0.1 fusion.11
  81.4 0.6 fusion.16
  82.0 102.3 %psum.7 = f32[]{:T(128)} all-reduce(f32[]{:T(128)} %fusion.16), channel_id=1, replica_groups=mesh['depth'=8,'tile'=64] {'depth','tile'}, use_global_device_ids=true, to_apply=%region_7.8 | all-reduce | flops 1 | bytes 8 | tf_op jit(solution)/shard_map/psum | solution.py:93
  185.0 0.6 maximum_bitcast_fusion
  (20 shorter events, 0.6 us)
Async XLA Ops:
  34.8 7.8 %collective-permute-start.1 = (f32[1,16,1024]{2,1,0:T(8,128)S(1)}, f32[1,16,1024]{2,1,0:T(8,128)S(1)}, u32[]{:S(2)}, u32[]{:S(2)}) collective-permute-start(f32[1,16,1024]{2,1,0:T(8,128)S(1)} %get-tuple-element.52), channel_id=1, source_target_pairs={{0,64},{64,128},{128,192},{192,256},{256,320},{320,384},{384,448},... | collective-permute-start | bytes 196616 | tf_op jit(solution)/shard_map/ppermute | solution.py:21
  38.9 5.0 %collective-permute-start = (f32[1,16,1024]{2,1,0:T(8,128)S(1)}, f32[1,16,1024]{2,1,0:T(8,128)S(1)}, u32[]{:S(2)}, u32[]{:S(2)}) collective-permute-start(f32[1,16,1024]{2,1,0:T(8,128)S(1)} %get-tuple-element.51), channel_id=1, source_target_pairs={{64,0},{128,64},{192,128},{256,192},{320,256},{384,320},{448,384},... | collective-permute-start | bytes 196616 | tf_op jit(solution)/shard_map/ppermute | solution.py:22
  44.6 15.2 %collective-permute-start.2 = (f32[10,1,1024]{2,1,0:T(1,128)}, f32[10,1,1024]{2,1,0:T(1,128)S(1)}, u32[]{:S(2)}, u32[]{:S(2)}) collective-permute-start(f32[10,1,1024]{2,1,0:T(1,128)} %get-tuple-element.54), channel_id=1, source_target_pairs={{1,0},{2,1},{3,2},{4,3},{5,4},{6,5},{7,6},{8,7},{9,8},{10,9},{11,1... | collective-permute-start | bytes 122888 | tf_op jit(solution)/shard_map/ppermute | solution.py:22
  51.7 8.0 %collective-permute-start.3 = (f32[10,1,1024]{2,1,0:T(1,128)S(1)}, f32[10,1,1024]{2,1,0:T(1,128)S(1)}, u32[]{:S(2)}, u32[]{:S(2)}) collective-permute-start(f32[10,1,1024]{2,1,0:T(1,128)S(1)} %get-tuple-element.53), channel_id=1, source_target_pairs={{0,1},{1,2},{2,3},{3,4},{4,5},{5,6},{6,7},{7,8},{8,9},{9,10},{10,1... | collective-permute-start | bytes 122888 | tf_op jit(solution)/shard_map/ppermute | solution.py:21
  56.7 3.0 %slice-start = ((f32[8,16,1024]{2,1,0:T(8,128)}), f32[7,16,1024]{2,1,0:T(8,128)S(1)}, s32[]{:S(2)}) async-start(f32[8,16,1024]{2,1,0:T(8,128)} %fusion.9), calls=%async_computation.1 | async-start | bytes 917504 | tf_op jit(solution)/shard_map/slice | solution.py:83
  59.7 1.0 copy-start
  61.6 0.8 slice-start.1
  62.4 6.1 %copy-start.1 = (s32[1,8]{1,0:T(1,128)S(1)}, s32[1,8]{1,0:T(1,128)}, u32[]{:S(2)}) copy-start(s32[1,8]{1,0:T(1,128)} %param.7) | copy-start | bytes 100
  63.5 17.4 %all-to-all-start = ((f32[4,8,2,1024]{3,2,0,1:T(2,128)}), f32[4,8,2,1024]{3,2,0,1:T(2,128)S(1)}, u32[]{:S(2)}, u32[]{:S(2)}) async-start(f32[4,8,2,1024]{3,2,0,1:T(2,128)} %copy.28), calls=%async_computation | async-start | bytes 524288 | tf_op jit(solution)/shard_map/all_to_all | solution.py:90
where the time goes:
time: 186 us
  blocking collectives  102 us (55%)
  matrix products  26.1 us (14%)
  starting transfers between devices  19.4 us (10%)
  local copies, waits for them, and re-layouts  15.5 us (8%)
  waiting for transfers between devices  13.2 us (7%)
  other arithmetic  8.13 us (4%)
    psum x1, blocking collectives, body(): log_sum = lax.psum(jnp.sum(jnp.log(0.05 + lum)), ('depth', 'tile'))  102 us
    dot_general x8, matrix products, one_block(): return jnp.dot(levels, onehot, preferred_element_type=jnp.float32)  26.1 us
    all_to_all x1, waiting for transfers between devices, body(): lax.all_to_all(stacked, 'depth', split_axis=1, concat_axis=1, tiled=True)  12.3 us
    ppermute x2, starting transfers between devices, padded_2(): after = lax.ppermute(initial, axis, down)  8.48 us
    ppermute x2, starting transfers between devices, padded_2(): before = lax.ppermute(last, axis, up)  5.95 us
    all_to_all x1, starting transfers between devices, body(): lax.all_to_all(stacked, 'depth', split_axis=1, concat_axis=1, tiled=True)  4.99 us
    slice x2, local copies, waits for them, and re-layouts, body(): colour = found[1:]  4.89 us
  transfers between devices with their start and end apart: 5, of which 2 were waited for; matrix products, arithmetic and copies ran while one was open for 5% of the time, Pallas kernels for 0%

commit v1 on v0

v1 whole, which is shorter than its diff:
```python
import functools
import math

import jax
import jax.numpy as jnp
from jax import lax
from jax.experimental import pallas as pl
from jax.experimental.pallas import tpu as pltpu
from jax.sharding import PartitionSpec as P

LIGHT_Z = 0.8
LIGHT_Y = 0.36
LIGHT_X = 0.48
KEY_VALUE = 0.18
INNER = 8
LANES = 128
SUBLANES = 8
MESH = pl.DeviceIdType.MESH


def gathered(table, index):
    return jnp.take_along_axis(table, index, axis=1, mode="promise_in_bounds")


def image_row(labels, z, y):
    blocks, depth_size, rows, lanes = labels.shape
    flat = labels.reshape(blocks * depth_size * rows, lanes)
    return flat[pl.ds(z * rows + y, blocks, stride=depth_size * rows), :]


def kernel(
    sizes,
    labels_hbm,
    order_hbm,
    opacity_hbm,
    colour_hbm,
    frame_ref,
    labels,
    order,
    opacity,
    colour,
    words,
    dens,
    diff_x,
    send_pass,
    send_colour,
    got_pass,
    got_colour,
    part_sums,
    inverse,
    load_sem,
    halo_send,
    halo_recv,
    pass_send,
    pass_recv,
    colour_send,
    colour_recv,
    sum_send,
    sum_recv,
):
    groups, strips, depth_size, rows = sizes
    inner = min(INNER, strips)
    outer = strips // inner
    cols = SUBLANES * LANES
    piece = rows // groups
    me = lax.axis_index("depth")
    tile = lax.axis_index("tile")
    tile_inner = lax.rem(tile, inner)
    tile_outer = tile // inner

    def partner(stage, offset):
        if stage == 0:
            return {"depth": lax.rem(me + offset, groups), "tile": tile}
        if stage == 1:
            return {"depth": me, "tile": tile_outer * inner + lax.rem(tile_inner + offset, inner)}
        return {"depth": me, "tile": lax.rem(tile_outer + offset, outer) * inner + tile_inner}

    stages = ((0, groups), (1, inner), (2, outer))

    loads = [
        pltpu.make_async_copy(
            labels_hbm.at[:, :, pl.ds(block * LANES, LANES)], labels.at[block], load_sem.at[block]
        )
        for block in range(SUBLANES)
    ]
    loads.append(pltpu.make_async_copy(opacity_hbm, opacity, load_sem.at[8]))
    loads.append(pltpu.make_async_copy(colour_hbm, colour, load_sem.at[9]))
    loads.append(pltpu.make_async_copy(order_hbm, order, load_sem.at[10]))
    for load in loads:
        load.start()

    barrier = pltpu.get_barrier_semaphore()
    for stage, count in stages:
        for offset in range(1, count):
            pl.semaphore_signal(
                barrier, inc=1, device_id=partner(stage, offset), device_id_type=MESH
            )
    has_up = tile < strips - 1
    has_down = tile > 0
    has_after = me < groups - 1
    has_before = me > 0

    @pl.when(has_up)
    def _():
        pl.semaphore_signal(
            barrier, inc=1, device_id={"depth": me, "tile": tile + 1}, device_id_type=MESH
        )

    @pl.when(has_down)
    def _():
        pl.semaphore_signal(
            barrier, inc=1, device_id={"depth": me, "tile": tile - 1}, device_id_type=MESH
        )

    for load in loads:
        load.wait()

    level = [opacity[...].reshape(1, 2 * LANES)] + [colour[c : c + 1, :] for c in range(3)]
    packed = level[0] + level[1] * 256 + level[2] * 65536 + level[3] * 16777216
    low = jnp.broadcast_to(packed[:, :LANES], (SUBLANES, LANES))
    high = jnp.broadcast_to(packed[:, LANES:], (SUBLANES, LANES))
    lane = lax.broadcasted_iota(jnp.int32, (SUBLANES, LANES), 1)
    sub = lax.broadcasted_iota(jnp.int32, (SUBLANES, LANES), 0)
    first_lane, last_lane = lane == 0, lane == LANES - 1
    first_cell = first_lane & (sub == 0)
    last_cell = last_lane & (sub == SUBLANES - 1)

    def look_up(z, carry):
        for y in range(rows):
            label = image_row(labels, z, y)
            index = label & (LANES - 1)
            word = jnp.where(label < LANES, gathered(low, index), gathered(high, index))
            words[z, y] = word
            value = (word & 255).astype(jnp.float32)
            dens[z + 1, y + 1] = value
            right = pltpu.roll(value, LANES - 1, 1)
            right = jnp.where(last_lane, pltpu.roll(right, SUBLANES - 1, 0), right)
            right = jnp.where(last_cell, 0.0, right)
            left = pltpu.roll(value, 1, 1)
            left = jnp.where(first_lane, pltpu.roll(left, 1, 0), left)
            left = jnp.where(first_cell, 0.0, left)
            diff_x[z, y] = right - left
        return carry

    lax.fori_loop(0, depth_size, look_up, 0)

    expected = sum(count - 1 for _, count in stages)
    pl.semaphore_wait(
        barrier, expected + has_up.astype(jnp.int32) + has_down.astype(jnp.int32)
    )

    def halo(kind):
        if kind == 0:
            src, dst = (depth_size, pl.ds(1, rows)), (0, pl.ds(1, rows))
            target = {"depth": me + 1, "tile": tile}
        elif kind == 1:
            src, dst = (1, pl.ds(1, rows)), (depth_size + 1, pl.ds(1, rows))
            target = {"depth": me - 1, "tile": tile}
        elif kind == 2:
            src, dst = (pl.ds(1, depth_size), rows), (pl.ds(1, depth_size), 0)
            target = {"depth": me, "tile": tile + 1}
        else:
            src, dst = (pl.ds(1, depth_size), 1), (pl.ds(1, depth_size), rows + 1)
            target = {"depth": me, "tile": tile - 1}
        return pltpu.make_async_remote_copy(
            src_ref=dens.at[src],
            dst_ref=dens.at[dst],
            send_sem=halo_send.at[kind],
            recv_sem=halo_recv.at[kind],
            device_id=target,
            device_id_type=MESH,
        )

    sends = (has_after, has_before, has_up, has_down)
    arrives = (has_before, has_after, has_down, has_up)
    for kind in range(4):

        @pl.when(sends[kind])
        def _(kind=kind):
            halo(kind).start()

    zero = jnp.zeros((SUBLANES, LANES), jnp.float32)

    @pl.when(jnp.logical_not(has_before))
    def _():
        for y in range(rows):
            dens[0, y + 1] = zero

    @pl.when(jnp.logical_not(has_after))
    def _():
        for y in range(rows):
            dens[depth_size + 1, y + 1] = zero

    @pl.when(jnp.logical_not(has_down))
    def _():
        for z in range(depth_size):
            dens[z + 1, 0] = zero

    @pl.when(jnp.logical_not(has_up))
    def _():
        for z in range(depth_size):
            dens[z + 1, rows + 1] = zero

    rate = -2.0 / (255.0 * depth_size * groups)

    def pass_copy(target, source):
        return pltpu.make_async_remote_copy(
            src_ref=send_pass.at[pl.ds(target * piece, piece)],
            dst_ref=got_pass.at[source],
            send_sem=pass_send.at[target],
            recv_sem=pass_recv.at[source],
            device_id={"depth": target, "tile": tile},
            device_id_type=MESH,
        )

    def colour_copy(target, source):
        return pltpu.make_async_remote_copy(
            src_ref=send_colour.at[pl.ds(target * piece, piece)],
            dst_ref=got_colour.at[source],
            send_sem=colour_send.at[target],
            recv_sem=colour_recv.at[source],
            device_id={"depth": target, "tile": tile},
            device_id_type=MESH,
        )

    def turn(step):
        half = (step + 1) // 2
        offset = groups // 2 + jnp.where(lax.rem(step, 2) == 0, half, -half)
        return lax.rem(me + offset + groups, groups)

    def do_pass(step, carry):
        target = turn(step)
        for r in range(piece):
            y = target * piece + r
            total = dens[1, y + 1]
            for z in range(1, depth_size):
                total = total + dens[z + 1, y + 1]
            send_pass[y] = jnp.exp(total * rate)

        @pl.when(target != me)
        def _():
            pass_copy(target, me).start()

        return carry

    lax.fori_loop(0, groups, do_pass, 0)

    for kind in range(4):

        @pl.when(arrives[kind])
        def _(kind=kind):
            halo(kind).wait_recv()

    def do_colour(step, carry):
        target = turn(step)
        for r in range(piece):
            y = target * piece + r
            total = jnp.zeros((SUBLANES, LANES), jnp.float32)
            through = jnp.ones((SUBLANES, LANES), jnp.float32)
            sums = [zero, zero, zero]
            for z in range(depth_size):
                word = words[z, y]
                total = total + dens[z + 1, y + 1]
                after = jnp.exp(total * rate)
                dz = dens[z + 2, y + 1] - dens[z, y + 1]
                dy = dens[z + 1, y + 2] - dens[z + 1, y]
                dx = diff_x[z, y]
                square = dz * dz + dy * dy + dx * dx
                toward = jnp.abs(
                    dz * (0.7 * LIGHT_Z) + dy * (0.7 * LIGHT_Y) + dx * (0.7 * LIGHT_X)
                )
                shade = 0.3 + toward * lax.rsqrt(jnp.maximum(square, (0.25 * 510.0) ** 2))
                weight = (through - after) * shade
                through = after
                for c in range(3):
                    part = lax.shift_right_logical(word, 8 * (c + 1))
                    if c < 2:
                        part = part & 255
                    sums[c] = sums[c] + part.astype(jnp.float32) * weight
            row = (tile * rows + y).astype(jnp.float32)
            ramp = (0.5 + (row + 0.5) / (rows * strips)) / 255.0
            for c in range(3):
                send_colour[y, c] = sums[c] * ramp

        @pl.when(target != me)
        def _():
            colour_copy(target, me).start()

        return carry

    lax.fori_loop(0, groups, do_colour, 0)

    for r in range(piece):
        got_pass[me, r] = send_pass[me * piece + r]
        for c in range(3):
            got_colour[me, r, c] = send_colour[me * piece + r, c]

    for rank in range(groups):
        at = 0
        for g in range(1, groups):
            at = jnp.where(order[0, g] == rank, g, at)
        inverse[rank] = at

    for offset in range(1, groups):
        source = lax.rem(me + offset, groups)
        pass_copy(source, source).wait_recv()
        colour_copy(source, source).wait_recv()

    composite = []
    ahead = []
    for r in range(piece):
        through = jnp.ones((SUBLANES, LANES), jnp.float32)
        sums = [zero, zero, zero]
        for rank in range(groups):
            g = inverse[rank]
            for c in range(3):
                sums[c] = sums[c] + through * got_colour[g, r, c]
            through = through * got_pass[g, r]
        composite.append(sums)
        ahead.append(through)

    logs = zero
    for r in range(piece):
        lum = 0.2126 * composite[r][0] + 0.7152 * composite[r][1] + 0.0722 * composite[r][2]
        logs = logs + jnp.log(0.05 + lum)
    local = jnp.sum(logs, axis=0, keepdims=True)

    for stage, count in stages:
        if count == 1:
            continue
        mine = (me, tile_inner, tile_outer)[stage]
        part_sums[stage, mine] = local

        def sum_copy(target, source, device, stage=stage):
            return pltpu.make_async_remote_copy(
                src_ref=part_sums.at[stage, source],
                dst_ref=part_sums.at[stage, source],
                send_sem=sum_send.at[stage, target],
                recv_sem=sum_recv.at[stage, source],
                device_id=device,
                device_id_type=MESH,
            )

        for offset in range(1, count):
            target = lax.rem(mine + offset, count)
            sum_copy(target, mine, partner(stage, offset)).start()
        for offset in range(1, count):
            source = lax.rem(mine + offset, count)
            sum_copy(source, source, partner(stage, offset)).wait_recv()
        local = part_sums[stage, 0]
        for source in range(1, count):
            local = local + part_sums[stage, source]
    log_sum = jnp.sum(local, axis=1, keepdims=True)
    scale = KEY_VALUE / jnp.exp(log_sum * (1.0 / (rows * strips * cols)))
    scale = jnp.broadcast_to(scale, (SUBLANES, LANES))

    for r in range(piece):
        for c in range(3):
            scaled = composite[r][c] * scale
            frame_ref[c, r] = scaled / (1.0 + scaled)
        frame_ref[3, r] = 1.0 - ahead[r]

    for kind in range(4):

        @pl.when(sends[kind])
        def _(kind=kind):
            halo(kind).wait_send()

    for offset in range(1, groups):
        target = lax.rem(me + offset, groups)
        pass_copy(target, me).wait_send()
        colour_copy(target, me).wait_send()
    for stage, count in stages:
        mine = (me, tile_inner, tile_outer)[stage]
        for offset in range(1, count):
            target = lax.rem(mine + offset, count)
            pltpu.make_async_remote_copy(
                src_ref=part_sums.at[stage, mine],
                dst_ref=part_sums.at[stage, mine],
                send_sem=sum_send.at[stage, target],
                recv_sem=sum_recv.at[stage, mine],
                device_id=partner(stage, offset),
                device_id_type=MESH,
            ).wait_send()


def body(labels, depth_order, opacity_table, colour_map):
    groups = lax.axis_size("depth")
    strips = lax.axis_size("tile")
    depth_size, rows, cols = labels.shape
    piece = rows // groups
    block = (SUBLANES, LANES)
    frame = pl.pallas_call(
        functools.partial(kernel, (groups, strips, depth_size, rows)),
        out_shape=jax.ShapeDtypeStruct((4, piece) + block, jnp.float32),
        in_specs=[pl.BlockSpec(memory_space=pl.ANY)] * 4,
        out_specs=pl.BlockSpec(memory_space=pltpu.VMEM),
        scratch_shapes=[
            pltpu.VMEM((SUBLANES, depth_size, rows, LANES), jnp.int32),
            pltpu.SMEM((1, groups), jnp.int32),
            pltpu.VMEM((2 * LANES,), jnp.int32),
            pltpu.VMEM((3, 2 * LANES), jnp.int32),
            pltpu.VMEM((depth_size, rows) + block, jnp.int32),
            pltpu.VMEM((depth_size + 2, rows + 2) + block, jnp.float32),
            pltpu.VMEM((depth_size, rows) + block, jnp.float32),
            pltpu.VMEM((rows,) + block, jnp.float32),
            pltpu.VMEM((rows, 3) + block, jnp.float32),
            pltpu.VMEM((groups, piece) + block, jnp.float32),
            pltpu.VMEM((groups, piece, 3) + block, jnp.float32),
            pltpu.VMEM((3, 8, 1, LANES), jnp.float32),
            pltpu.SMEM((groups,), jnp.int32),
            pltpu.SemaphoreType.DMA((11,)),
            pltpu.SemaphoreType.DMA((4,)),
            pltpu.SemaphoreType.DMA((4,)),
            pltpu.SemaphoreType.DMA((groups,)),
            pltpu.SemaphoreType.DMA((groups,)),
            pltpu.SemaphoreType.DMA((groups,)),
            pltpu.SemaphoreType.DMA((groups,)),
            pltpu.SemaphoreType.DMA((3, 8)),
            pltpu.SemaphoreType.DMA((3, 8)),
        ],
        compiler_params=pltpu.CompilerParams(
            collective_id=0, has_side_effects=True, vmem_limit_bytes=60 * 1024 * 1024
        ),
        name="render",
    )(labels, depth_order, opacity_table, colour_map)
    return frame.reshape(4, 1, piece, cols)


def solution(mesh):
    in_specs = (P("depth", "tile", None), P("tile", None), P(), P())
    out_specs = P(None, "tile", "depth", None)
    return jax.shard_map(body, mesh=mesh, in_specs=in_specs, out_specs=out_specs, check_vma=False)
```

time: 186 us -> 39.3 us (0.21)
  blocking collectives: 102 us -> 0 us
  Pallas kernels: 0 us -> 37.7 us
  matrix products: 26.1 us -> 0 us
  starting transfers between devices: 19.4 us -> 0 us
  local copies, waits for them, and re-layouts: 15.5 us -> 1.39 us
  waiting for transfers between devices: 13.2 us -> 0 us
  other arithmetic: 8.13 us -> 0 us
    psum x1 -> x0, blocking collectives: 102 us -> none  [body(): log_sum = lax.psum(jnp.sum(jnp.log(0.05 + lum)), ('depth', 'tile'))]
    pallas_call x0 -> x1, Pallas kernels: none -> 37.7 us  [body(): pl.pallas_call(functools.partial(kernel, (groups, strips, depth_size, row...]
    dot_general x8 -> x0, matrix products: 26.1 us -> none  [one_block(): return jnp.dot(levels, onehot, preferred_element_type=jnp.float32)]
    ppermute x4 -> x0, starting transfers between devices: 14.4 us -> none  [the longest x2 8.48 us: padded_2(): after = lax.ppermute(initial, axis, down)]
    all_to_all x1 -> x0, waiting for transfers between devices: 12.3 us -> none  [body(): lax.all_to_all(stacked, 'depth', split_axis=1, concat_axis=1, tiled=True)]
    slice x9 -> x0, local copies, waits for them, and re-layouts: 8.32 us -> none  [the longest x2 4.89 us: body(): colour = found[1:]]
    all_to_all x1 -> x0, starting transfers between devices: 4.99 us -> none  [body(): lax.all_to_all(stacked, 'depth', split_axis=1, concat_axis=1, tiled=True)]
    unnamed x8 -> x0, local copies, waits for them, and re-layouts: 3.18 us -> none
  transfers between devices with their start and end apart: 5 -> 0, of which waited for: 2 -> 0; matrix products, arithmetic and copies ran while one was open for 5% -> 0% of each run, Pallas kernels for 0% -> 0%
where the time goes in v1:
time: 39.3 us; the launch traced here: 39.1 us
  Pallas kernels  37.7 us (96%)
  local copies, waits for them, and re-layouts  1.39 us (4%)
    pallas_call x1, Pallas kernels, body(): pl.pallas_call(functools.partial(kernel, (groups, strips, depth_size, row...  37.7 us
    reshape x1, local copies, waits for them, and re-layouts, body(): return frame.reshape(4, 1, piece, cols)  1.39 us

profile of v1, /device:TPU:1, one launch (start us, length us, event | category | flops | bytes accessed | tf_op | source)
XLA Modules:
  0.0 39.1 jit_solution(7148525668644587734)
XLA Ops:
  0.0 37.7 %render.1 = f32[4,2,8,128]{3,2,1,0:T(8,128)} custom-call(s32[8,16,1024]{2,1,0:T(8,128)} %labels_hbm.1, s32[1,8]{1,0:T(1,128)} %order_hbm.1, s32[256]{0:T(256)} %opacity_hbm.1, s32[3,256]{1,0:T(4,128)} %colour_hbm.1), custom_call_target="tpu_custom_call" | custom-call | tf_op jit(solution)/shard_map/render/pallas_call | solution.py:393
  37.7 1.4 %reshape.3 = f32[4,1,2,1024]{3,2,0,1:T(2,128)} reshape(f32[4,2,8,128]{3,2,1,0:T(8,128)} %render.1) | data formatting | bytes 65536 | tf_op jit(solution)/shard_map/reshape | solution.py:427

commit v2 on v1

v2 whole, which is shorter than its diff:
```python
import functools

import jax
import jax.numpy as jnp
from jax import lax
from jax.experimental import pallas as pl
from jax.experimental.pallas import tpu as pltpu
from jax.sharding import PartitionSpec as P

LIGHT_Z = 0.8
LIGHT_Y = 0.36
LIGHT_X = 0.48
KEY_VALUE = 0.18
SIZE_X = 4
LANES = 128
SUBLANES = 8
MESH = pl.DeviceIdType.MESH


def gathered(table, index):
    return jnp.take_along_axis(table, index, axis=1, mode="promise_in_bounds")


def image_row(labels, z, y):
    blocks, depth_size, rows, lanes = labels.shape
    flat = labels.reshape(blocks * depth_size * rows, lanes)
    return flat[pl.ds(z * rows + y, blocks, stride=depth_size * rows), :]


def kernel(
    sizes,
    labels_hbm,
    order_hbm,
    opacity_hbm,
    colour_hbm,
    frame_ref,
    labels,
    order,
    opacity,
    colour,
    words,
    dens,
    send_pass,
    send_colour,
    got_pass,
    got_colour,
    part_one,
    part_two,
    inverse,
    load_sem,
    halo_send,
    halo_recv,
    block_send,
    block_recv,
    sum_send,
    sum_recv,
    rounds,
):
    groups, strips, depth_size, rows = sizes
    cols = SUBLANES * LANES
    piece = rows // groups
    size_x = min(SIZE_X, strips // 2)
    size_z = strips // (2 * size_x)
    me = lax.axis_index("depth")
    tile = lax.axis_index("tile")
    chip = tile // 2
    core = lax.rem(tile, 2)
    at_x = lax.rem(chip, size_x)
    at_z = chip // size_x
    lengths = {"y": groups, "x": size_x, "z": size_z}

    def along(axis, offset):
        if axis == "y":
            return {"depth": lax.rem(me + offset, groups), "tile": tile}
        if axis == "x":
            there = at_z * size_x + lax.rem(at_x + offset, size_x)
        else:
            there = lax.rem(at_z + offset, size_z) * size_x + at_x
        return {"depth": me, "tile": there * 2 + core}

    def greet(semaphore, device):
        pl.semaphore_signal(semaphore, inc=1, device_id=device, device_id_type=MESH)

    barrier = pltpu.get_barrier_semaphore()
    has_up = tile < strips - 1
    has_down = tile > 0
    has_after = me < groups - 1
    has_before = me > 0
    other_core = {"depth": me, "tile": tile + 1 - 2 * core}
    near = [(a, o) for a, n in lengths.items() if n > 1 for o in sorted({1, n - 1})]
    for axis, offset in near:
        greet(barrier, along(axis, offset))
    greet(barrier, other_core)
    beside = jnp.where(core == 0, tile - 1, tile + 1)
    has_beside = (beside >= 0) & (beside < strips)

    @pl.when(has_beside)
    def _():
        greet(barrier, {"depth": me, "tile": beside})

    for block in range(SUBLANES):
        pltpu.make_async_copy(
            labels_hbm.at[:, :, pl.ds(block * LANES, LANES)], labels.at[block], load_sem.at[0]
        ).start()
    loads = [
        pltpu.make_async_copy(opacity_hbm, opacity, load_sem.at[1]),
        pltpu.make_async_copy(colour_hbm, colour, load_sem.at[2]),
        pltpu.make_async_copy(order_hbm, order, load_sem.at[3]),
    ]
    for load in loads:
        load.start()
    for load in loads:
        load.wait()

    level = [opacity[...].reshape(1, 2 * LANES)] + [colour[c : c + 1, :] for c in range(3)]
    packed = level[0] + level[1] * 256 + level[2] * 65536 + level[3] * 16777216
    low = jnp.broadcast_to(packed[:, :LANES], (SUBLANES, LANES))
    high = jnp.broadcast_to(packed[:, LANES:], (SUBLANES, LANES))
    lane = lax.broadcasted_iota(jnp.int32, (SUBLANES, LANES), 1)
    sub = lax.broadcasted_iota(jnp.int32, (SUBLANES, LANES), 0)
    first_lane, last_lane = lane == 0, lane == LANES - 1
    first_cell = first_lane & (sub == 0)
    last_cell = last_lane & (sub == SUBLANES - 1)
    zero = jnp.zeros((SUBLANES, LANES), jnp.float32)
    one = jnp.ones((SUBLANES, LANES), jnp.float32)
    pltpu.make_async_copy(labels, labels, load_sem.at[0]).wait()

    def look_up(z, y):
        label = image_row(labels, z, y)
        index = label & (LANES - 1)
        word = jnp.where(label < LANES, gathered(low, index), gathered(high, index))
        words[z, y] = word
        dens[z + 1, y + 1] = (word & 255).astype(jnp.float32)

    def halo(kind):
        if kind == 0:
            src, dst = (depth_size, pl.ds(1, rows)), (0, pl.ds(1, rows))
            target = {"depth": me + 1, "tile": tile}
        elif kind == 1:
            src, dst = (1, pl.ds(1, rows)), (depth_size + 1, pl.ds(1, rows))
            target = {"depth": me - 1, "tile": tile}
        elif kind == 2:
            src, dst = (pl.ds(1, depth_size), rows), (pl.ds(1, depth_size), 0)
            target = {"depth": me, "tile": tile + 1}
        else:
            src, dst = (pl.ds(1, depth_size), 1), (pl.ds(1, depth_size), rows + 1)
            target = {"depth": me, "tile": tile - 1}
        return pltpu.make_async_remote_copy(
            src_ref=dens.at[src],
            dst_ref=dens.at[dst],
            send_sem=halo_send.at[kind],
            recv_sem=halo_recv.at[kind],
            device_id=target,
            device_id_type=MESH,
        )

    sends = (has_after, has_before, has_up, has_down)
    arrives = (has_before, has_after, has_down, has_up)

    def start_halo(kind):
        @pl.when(sends[kind])
        def _():
            halo(kind).start()

    for y in range(rows):
        look_up(depth_size - 1, y)
        look_up(0, y)
    pl.semaphore_wait(barrier, len(near) + 1 + has_beside.astype(jnp.int32))
    start_halo(0)
    start_halo(1)
    first_round = [(a, o) for a, o in near if lengths[a] >= 4]
    for axis, offset in first_round:
        greet(rounds.at[0], along(axis, offset))
    for z in range(1, depth_size - 1):
        look_up(z, 0)
        look_up(z, rows - 1)
    start_halo(2)
    start_halo(3)

    @pl.when(jnp.logical_not(has_before))
    def _():
        for y in range(rows):
            dens[0, y + 1] = zero

    @pl.when(jnp.logical_not(has_after))
    def _():
        for y in range(rows):
            dens[depth_size + 1, y + 1] = zero

    @pl.when(jnp.logical_not(has_down))
    def _():
        for z in range(depth_size):
            dens[z + 1, 0] = zero

    @pl.when(jnp.logical_not(has_up))
    def _():
        for z in range(depth_size):
            dens[z + 1, rows + 1] = zero

    def look_up_layer(z, carry):
        for y in range(1, rows - 1):
            look_up(z, y)
        return carry

    lax.fori_loop(1, depth_size - 1, look_up_layer, 0)

    rate = -2.0 / (255.0 * depth_size * groups)
    for y in range(rows):
        total = dens[1, y + 1]
        for z in range(1, depth_size):
            total = total + dens[z + 1, y + 1]
        send_pass[y] = jnp.exp(total * rate)

    if first_round:
        pl.semaphore_wait(rounds.at[0], len(first_round))
    second_round = [(a, o) for a, n in lengths.items() if n >= 8 for o in (2, n - 2)]
    for axis, offset in second_round:
        greet(rounds.at[1], along(axis, offset))
    if second_round:
        pl.semaphore_wait(rounds.at[1], len(second_round))
    third_round = [("x", o) for o in range(1, size_x)] if size_z > 1 else []
    for axis, offset in third_round:
        greet(rounds.at[2], along(axis, offset))

    def block_copy(sent, got, which, target):
        return pltpu.make_async_remote_copy(
            src_ref=sent.at[pl.ds(target * piece, piece)],
            dst_ref=got.at[me],
            send_sem=block_send.at[which],
            recv_sem=block_recv.at[which],
            device_id={"depth": target, "tile": tile},
            device_id_type=MESH,
        )

    def turn(step):
        half = (step + 1) // 2
        offset = groups // 2 + jnp.where(lax.rem(step, 2) == 0, half, -half)
        return lax.rem(me + offset + groups, groups)

    def pass_block(step, carry):
        block_copy(send_pass, got_pass, 0, turn(step)).start()
        return carry

    lax.fori_loop(0, groups - 1, pass_block, 0)

    for kind in range(4):

        @pl.when(arrives[kind])
        def _(kind=kind):
            halo(kind).wait_recv()

    def do_colour(step, carry):
        target = turn(step)
        for r in range(piece):
            y = target * piece + r
            total = zero
            through = one
            sums = [zero, zero, zero]
            for z in range(depth_size):
                word = words[z, y]
                value = dens[z + 1, y + 1]
                total = total + value
                after = jnp.exp(total * rate)
                right = pltpu.roll(value, LANES - 1, 1)
                right = jnp.where(last_lane, pltpu.roll(right, SUBLANES - 1, 0), right)
                right = jnp.where(last_cell, 0.0, right)
                left = pltpu.roll(value, 1, 1)
                left = jnp.where(first_lane, pltpu.roll(left, 1, 0), left)
                left = jnp.where(first_cell, 0.0, left)
                dz = dens[z + 2, y + 1] - dens[z, y + 1]
                dy = dens[z + 1, y + 2] - dens[z + 1, y]
                dx = right - left
                square = dz * dz + dy * dy + dx * dx
                toward = jnp.abs(
                    dz * (0.7 * LIGHT_Z) + dy * (0.7 * LIGHT_Y) + dx * (0.7 * LIGHT_X)
                )
                shade = 0.3 + toward * lax.rsqrt(jnp.maximum(square, (0.25 * 510.0) ** 2))
                weight = (through - after) * shade
                through = after
                for c in range(3):
                    part = lax.shift_right_logical(word, 8 * (c + 1))
                    if c < 2:
                        part = part & 255
                    sums[c] = sums[c] + part.astype(jnp.float32) * weight
            row = (tile * rows + y).astype(jnp.float32)
            ramp = (0.5 + (row + 0.5) / (rows * strips)) / 255.0
            for c in range(3):
                send_colour[y, c] = sums[c] * ramp

        @pl.when(target != me)
        def _():
            block_copy(send_colour, got_colour, 1, target).start()

        return carry

    lax.fori_loop(0, groups, do_colour, 0)

    for r in range(piece):
        got_pass[me, r] = send_pass[me * piece + r]
        for c in range(3):
            got_colour[me, r, c] = send_colour[me * piece + r, c]

    for rank in range(groups):
        at = 0
        for g in range(1, groups):
            at = jnp.where(order[0, g] == rank, g, at)
        inverse[rank] = at

    if third_round:
        pl.semaphore_wait(rounds.at[2], len(third_round))

    def all_but_one(ref, semaphore):
        part = ref.at[pl.ds(0, ref.shape[0] - 1)]
        return pltpu.make_async_copy(part, part, semaphore)

    all_but_one(got_pass, block_recv.at[0]).wait()
    all_but_one(got_colour, block_recv.at[1]).wait()

    composite = []
    ahead = []
    for r in range(piece):
        through = one
        sums = [zero, zero, zero]
        for rank in range(groups):
            g = inverse[rank]
            for c in range(3):
                sums[c] = sums[c] + through * got_colour[g, r, c]
            through = through * got_pass[g, r]
        composite.append(sums)
        ahead.append(through)

    logs = zero
    for r in range(piece):
        lum = 0.2126 * composite[r][0] + 0.7152 * composite[r][1] + 0.0722 * composite[r][2]
        logs = logs + jnp.log(0.05 + lum)
    local = jnp.sum(logs, axis=0, keepdims=True)

    def in_first(index):
        return {"depth": index // 2, "tile": chip * 2 + lax.rem(index, 2)}

    def in_second(index):
        return {"depth": me, "tile": index * 2 + core}

    stages = ((part_one, me * 2 + core, in_first), (part_two, chip, in_second))
    for stage, (parts, mine, device) in enumerate(stages):
        count = parts.shape[0]
        parts[mine] = local
        for offset in range(1, count):
            pltpu.make_async_remote_copy(
                src_ref=parts.at[mine],
                dst_ref=parts.at[mine],
                send_sem=sum_send.at[stage],
                recv_sem=sum_recv.at[stage],
                device_id=device(lax.rem(mine + offset, count)),
                device_id_type=MESH,
            ).start()
        all_but_one(parts, sum_recv.at[stage]).wait()
        local = jnp.sum(parts[...], axis=0)
    log_sum = jnp.sum(local, axis=1, keepdims=True)
    scale = KEY_VALUE / jnp.exp(log_sum * (1.0 / (rows * strips * cols)))
    scale = jnp.broadcast_to(scale, (SUBLANES, LANES))

    for r in range(piece):
        for c in range(3):
            scaled = composite[r][c] * scale
            frame_ref[c, r] = scaled / (1.0 + scaled)
        frame_ref[3, r] = 1.0 - ahead[r]

    for kind in range(4):

        @pl.when(sends[kind])
        def _(kind=kind):
            halo(kind).wait_send()

    all_but_one(got_pass, block_send.at[0]).wait()
    all_but_one(got_colour, block_send.at[1]).wait()
    all_but_one(part_one, sum_send.at[0]).wait()
    all_but_one(part_two, sum_send.at[1]).wait()


def body(labels, depth_order, opacity_table, colour_map):
    groups = lax.axis_size("depth")
    strips = lax.axis_size("tile")
    depth_size, rows, cols = labels.shape
    piece = rows // groups
    block = (SUBLANES, LANES)
    frame = pl.pallas_call(
        functools.partial(kernel, (groups, strips, depth_size, rows)),
        out_shape=jax.ShapeDtypeStruct((4, piece) + block, jnp.float32),
        in_specs=[pl.BlockSpec(memory_space=pl.ANY)] * 4,
        out_specs=pl.BlockSpec(memory_space=pltpu.VMEM),
        scratch_shapes=[
            pltpu.VMEM((SUBLANES, depth_size, rows, LANES), jnp.int32),
            pltpu.SMEM((1, groups), jnp.int32),
            pltpu.VMEM((2 * LANES,), jnp.int32),
            pltpu.VMEM((3, 2 * LANES), jnp.int32),
            pltpu.VMEM((depth_size, rows) + block, jnp.int32),
            pltpu.VMEM((depth_size + 2, rows + 2) + block, jnp.float32),
            pltpu.VMEM((rows,) + block, jnp.float32),
            pltpu.VMEM((rows, 3) + block, jnp.float32),
            pltpu.VMEM((groups, piece) + block, jnp.float32),
            pltpu.VMEM((groups, piece, 3) + block, jnp.float32),
            pltpu.VMEM((groups * 2, 1, LANES), jnp.float32),
            pltpu.VMEM((strips // 2, 1, LANES), jnp.float32),
            pltpu.SMEM((groups,), jnp.int32),
            pltpu.SemaphoreType.DMA((4,)),
            pltpu.SemaphoreType.DMA((4,)),
            pltpu.SemaphoreType.DMA((4,)),
            pltpu.SemaphoreType.DMA((2,)),
            pltpu.SemaphoreType.DMA((2,)),
            pltpu.SemaphoreType.DMA((2,)),
            pltpu.SemaphoreType.DMA((2,)),
            pltpu.SemaphoreType.REGULAR((3,)),
        ],
        compiler_params=pltpu.CompilerParams(
            collective_id=0, has_side_effects=True, vmem_limit_bytes=60 * 1024 * 1024
        ),
        name="render",
    )(labels, depth_order, opacity_table, colour_map)
    return frame.reshape(4, 1, piece, cols)


def solution(mesh):
    in_specs = (P("depth", "tile", None), P("tile", None), P(), P())
    out_specs = P(None, "tile", "depth", None)
    return jax.shard_map(body, mesh=mesh, in_specs=in_specs, out_specs=out_specs, check_vma=False)
```

time: 39.3 us -> 36.7 us (0.934)
  Pallas kernels: 37.7 us -> 35.1 us
    pallas_call x1, Pallas kernels: 37.7 us -> 35.1 us  [body(): pl.pallas_call(functools.partial(kernel, (groups, strips, depth_size, row...]
where the time goes in v2:
time: 36.7 us; the launch traced here: 36.5 us
  Pallas kernels  35.1 us (96%)
  local copies, waits for them, and re-layouts  1.39 us (4%)
    pallas_call x1, Pallas kernels, body(): pl.pallas_call(functools.partial(kernel, (groups, strips, depth_size, row...  35.1 us
    reshape x1, local copies, waits for them, and re-layouts, body(): return frame.reshape(4, 1, piece, cols)  1.39 us

profile of v2, /device:TPU:1, one launch (start us, length us, event | category | flops | bytes accessed | tf_op | source)
XLA Modules:
  0.0 36.5 jit_solution(14284776625764695236)
XLA Ops:
  0.0 35.1 %render.1 = f32[4,2,8,128]{3,2,1,0:T(8,128)} custom-call(s32[8,16,1024]{2,1,0:T(8,128)} %labels_hbm.1, s32[1,8]{1,0:T(1,128)} %order_hbm.1, s32[256]{0:T(256)} %opacity_hbm.1, s32[3,256]{1,0:T(4,128)} %colour_hbm.1), custom_call_target="tpu_custom_call" | custom-call | tf_op jit(solution)/shard_map/render/pallas_call | solution.py:387
  35.1 1.4 %reshape.3 = f32[4,1,2,1024]{3,2,0,1:T(2,128)} reshape(f32[4,2,8,128]{3,2,1,0:T(8,128)} %render.1) | data formatting | bytes 65536 | tf_op jit(solution)/shard_map/reshape | solution.py:420

commit v3 on v2

--- a/solution.py
+++ b/solution.py
@@ -363,8 +363,8 @@
     for r in range(piece):
         for c in range(3):
             scaled = composite[r][c] * scale
-            frame_ref[c, r] = scaled / (1.0 + scaled)
-        frame_ref[3, r] = 1.0 - ahead[r]
+            frame_ref[c, :, r, :] = scaled / (1.0 + scaled)
+        frame_ref[3, :, r, :] = 1.0 - ahead[r]
 
     for kind in range(4):
 
@@ -386,7 +386,7 @@
     block = (SUBLANES, LANES)
     frame = pl.pallas_call(
         functools.partial(kernel, (groups, strips, depth_size, rows)),
-        out_shape=jax.ShapeDtypeStruct((4, piece) + block, jnp.float32),
+        out_shape=pltpu.VMEM((4, SUBLANES, piece, LANES), jnp.float32),
         in_specs=[pl.BlockSpec(memory_space=pl.ANY)] * 4,
         out_specs=pl.BlockSpec(memory_space=pltpu.VMEM),
         scratch_shapes=[
@@ -413,11 +413,11 @@
             pltpu.SemaphoreType.REGULAR((3,)),
         ],
         compiler_params=pltpu.CompilerParams(
-            collective_id=0, has_side_effects=True, vmem_limit_bytes=60 * 1024 * 1024
+            collective_id=0, has_side_effects=True, vmem_limit_bytes=32 * 1024 * 1024
         ),
         name="render",
-    )(labels, depth_order, opacity_table, colour_map)
-    return frame.reshape(4, 1, piece, cols)
+    )(*[pltpu.with_memory_space_constraint(a, pltpu.HBM) for a in (labels, depth_order, opacity_table, colour_map)])
+    return jnp.swapaxes(frame, 1, 2).reshape(4, 1, piece, cols)
 
 
 def solution(mesh):

time: 36.7 us -> 35.3 us (0.962)
  local copies, waits for them, and re-layouts: 1.39 us -> 0.62 us
  Pallas kernels: 35.1 us -> 34.5 us
    reshape x1 -> x0, local copies, waits for them, and re-layouts: 1.39 us -> none  [body(): return frame.reshape(4, 1, piece, cols)]
    unnamed x0 -> x1, local copies, waits for them, and re-layouts: none -> 0.62 us
    pallas_call x1, Pallas kernels: 35.1 us -> 34.5 us  [body(): pl.pallas_call(functools.partial(kernel, (groups, strips, depth_size, row...]
where the time goes in v3:
time: 35.3 us; the launch traced here: 35.1 us
  Pallas kernels  34.5 us (98%)
  local copies, waits for them, and re-layouts  0.62 us (2%)
    pallas_call x1, Pallas kernels, body(): pl.pallas_call(functools.partial(kernel, (groups, strips, depth_size, row...  34.5 us

profile of v3, /device:TPU:1, one launch (start us, length us, event | category | flops | bytes accessed | tf_op | source)
XLA Modules:
  0.0 35.1 jit_solution(18229734236182334603)
XLA Ops:
  0.0 34.5 %render.1 = f32[4,8,2,128]{3,2,1,0:T(2,128)S(1)} custom-call(s32[8,16,1024]{2,1,0:T(8,128)} %labels_hbm.1, s32[1,8]{1,0:T(1,128)} %order_hbm.1, s32[256]{0:T(256)} %opacity_hbm.1, s32[3,256]{1,0:T(4,128)} %colour_hbm.1), custom_call_target="tpu_custom_call" | custom-call | tf_op jit(solution)/shard_map/render/pallas_call | solution.py:387
  34.5 0.6 %copy.6 = f32[4,1,2,1024]{3,2,1,0:T(2,128)} copy(f32[4,1,2,1024]{3,2,1,0:T(2,128)S(1)} %bitcast.3) | data formatting | bytes 65536

commit v4 on v3

--- a/solution.py
+++ b/solution.py
@@ -49,7 +49,8 @@
     inverse,
     load_sem,
     halo_send,
-    halo_recv,
+    layer_recv,
+    row_recv,
     block_send,
     block_recv,
     sum_send,
@@ -63,19 +64,19 @@
     size_z = strips // (2 * size_x)
     me = lax.axis_index("depth")
     tile = lax.axis_index("tile")
-    chip = tile // 2
-    core = lax.rem(tile, 2)
-    at_x = lax.rem(chip, size_x)
-    at_z = chip // size_x
+    chip = tile >> 1
+    core = tile & 1
+    at_x = chip & (size_x - 1)
+    at_z = lax.div(chip, size_x)
     lengths = {"y": groups, "x": size_x, "z": size_z}
 
     def along(axis, offset):
         if axis == "y":
-            return {"depth": lax.rem(me + offset, groups), "tile": tile}
+            return {"depth": (me + offset) & (groups - 1), "tile": tile}
         if axis == "x":
-            there = at_z * size_x + lax.rem(at_x + offset, size_x)
+            there = at_z * size_x + ((at_x + offset) & (size_x - 1))
         else:
-            there = lax.rem(at_z + offset, size_z) * size_x + at_x
+            there = ((at_z + offset) & (size_z - 1)) * size_x + at_x
         return {"depth": me, "tile": there * 2 + core}
 
     def greet(semaphore, device):
@@ -93,10 +94,12 @@
     greet(barrier, other_core)
     beside = jnp.where(core == 0, tile - 1, tile + 1)
     has_beside = (beside >= 0) & (beside < strips)
-
-    @pl.when(has_beside)
-    def _():
-        greet(barrier, {"depth": me, "tile": beside})
+    beside_near = jnp.where(core == 0, at_x > 0, at_x < size_x - 1)
+    beside_far = jnp.logical_and(has_beside, jnp.logical_not(beside_near))
+
+    next_x = (at_x + 2 * core - 1) & (size_x - 1)
+    across = {"depth": me, "tile": (at_z * size_x + next_x) * 2 + 1 - core}
+    greet(barrier, across)
 
     for block in range(SUBLANES):
         pltpu.make_async_copy(
@@ -132,50 +135,74 @@
         words[z, y] = word
         dens[z + 1, y + 1] = (word & 255).astype(jnp.float32)
 
-    def halo(kind):
-        if kind == 0:
-            src, dst = (depth_size, pl.ds(1, rows)), (0, pl.ds(1, rows))
-            target = {"depth": me + 1, "tile": tile}
-        elif kind == 1:
-            src, dst = (1, pl.ds(1, rows)), (depth_size + 1, pl.ds(1, rows))
-            target = {"depth": me - 1, "tile": tile}
-        elif kind == 2:
-            src, dst = (pl.ds(1, depth_size), rows), (pl.ds(1, depth_size), 0)
-            target = {"depth": me, "tile": tile + 1}
-        else:
-            src, dst = (pl.ds(1, depth_size), 1), (pl.ds(1, depth_size), rows + 1)
-            target = {"depth": me, "tile": tile - 1}
+    def block_at(depth, step):
+        inner = groups - 2
+        turn = depth + groups // 2 - 1 + step
+        for _ in range(2):
+            turn = jnp.where(turn >= inner, turn - inner, turn)
+        swap = (depth < groups // 2).astype(jnp.int32)
+        last = jnp.where(step - inner == swap, 0, groups - 1)
+        return jnp.where(step < inner, turn + 1, last)
+
+    def start_layer(kind):
+        target = me + 1 if kind == 0 else me - 1
+        src, dst = (depth_size, 0) if kind == 0 else (1, depth_size + 1)
+        for step in range(groups):
+            part = pl.ds(block_at(target, step) * piece + 1, piece)
+            pltpu.make_async_remote_copy(
+                src_ref=dens.at[src, part],
+                dst_ref=dens.at[dst, part],
+                send_sem=halo_send.at[kind],
+                recv_sem=layer_recv.at[kind, step // 2],
+                device_id={"depth": target, "tile": tile},
+                device_id_type=MESH,
+            ).start()
+
+    def rows_copy(count, semaphore):
+        part = dens.at[0, pl.ds(0, count)]
+        return pltpu.make_async_copy(part, part, semaphore)
+
+    def row_copy(up):
+        row, there = (rows, 0) if up else (1, rows + 1)
         return pltpu.make_async_remote_copy(
-            src_ref=dens.at[src],
-            dst_ref=dens.at[dst],
-            send_sem=halo_send.at[kind],
-            recv_sem=halo_recv.at[kind],
-            device_id=target,
+            src_ref=dens.at[pl.ds(1, depth_size), row],
+            dst_ref=dens.at[pl.ds(1, depth_size), there],
+            send_sem=halo_send.at[2 if up else 3],
+            recv_sem=row_recv.at[0 if up else 1],
+            device_id={"depth": me, "tile": tile + 1 if up else tile - 1},
             device_id_type=MESH,
         )
 
+    def start_row(up, condition):
+        @pl.when(condition)
+        def _():
+            row_copy(up).start()
+
     sends = (has_after, has_before, has_up, has_down)
-    arrives = (has_before, has_after, has_down, has_up)
-
-    def start_halo(kind):
-        @pl.when(sends[kind])
-        def _():
-            halo(kind).start()
 
     for y in range(rows):
         look_up(depth_size - 1, y)
         look_up(0, y)
-    pl.semaphore_wait(barrier, len(near) + 1 + has_beside.astype(jnp.int32))
-    start_halo(0)
-    start_halo(1)
+    pl.semaphore_wait(barrier, len(near) + 2)
+
+    @pl.when(has_after)
+    def _():
+        start_layer(0)
+
+    @pl.when(has_before)
+    def _():
+        start_layer(1)
+
     first_round = [(a, o) for a, o in near if lengths[a] >= 4]
     for axis, offset in first_round:
         greet(rounds.at[0], along(axis, offset))
+    if size_z > 1:
+        greet(rounds.at[0], across)
     for z in range(1, depth_size - 1):
         look_up(z, 0)
         look_up(z, rows - 1)
-    start_halo(2)
-    start_halo(3)
+    start_row(True, (core == 0) | beside_near)
+    start_row(False, (core == 1) | beside_near)
 
     @pl.when(jnp.logical_not(has_before))
     def _():
@@ -210,17 +237,6 @@
         for z in range(1, depth_size):
             total = total + dens[z + 1, y + 1]
         send_pass[y] = jnp.exp(total * rate)
-
-    if first_round:
-        pl.semaphore_wait(rounds.at[0], len(first_round))
-    second_round = [(a, o) for a, n in lengths.items() if n >= 8 for o in (2, n - 2)]
-    for axis, offset in second_round:
-        greet(rounds.at[1], along(axis, offset))
-    if second_round:
-        pl.semaphore_wait(rounds.at[1], len(second_round))
-    third_round = [("x", o) for o in range(1, size_x)] if size_z > 1 else []
-    for axis, offset in third_round:
-        greet(rounds.at[2], along(axis, offset))
 
     def block_copy(sent, got, which, target):
         return pltpu.make_async_remote_copy(
@@ -232,25 +248,25 @@
             device_id_type=MESH,
         )
 
-    def turn(step):
-        half = (step + 1) // 2
-        offset = groups // 2 + jnp.where(lax.rem(step, 2) == 0, half, -half)
-        return lax.rem(me + offset + groups, groups)
-
-    def pass_block(step, carry):
-        block_copy(send_pass, got_pass, 0, turn(step)).start()
-        return carry
-
-    lax.fori_loop(0, groups - 1, pass_block, 0)
-
-    for kind in range(4):
-
-        @pl.when(arrives[kind])
-        def _(kind=kind):
-            halo(kind).wait_recv()
-
-    def do_colour(step, carry):
-        target = turn(step)
+    def send_passes(offsets):
+        for offset in offsets:
+            block_copy(send_pass, got_pass, 0, (me + offset) & (groups - 1)).start()
+
+    pl.semaphore_wait(rounds.at[0], len(first_round) + (size_z > 1))
+    second_round = [(a, o) for a, n in lengths.items() if n >= 8 for o in (2, n - 2)]
+    for axis, offset in second_round:
+        greet(rounds.at[1], along(axis, offset))
+    start_row(True, (core == 1) & beside_far)
+    start_row(False, (core == 0) & beside_far)
+    send_passes((2, groups - 2, 1, groups - 1))
+    if second_round:
+        pl.semaphore_wait(rounds.at[1], len(second_round))
+    third_round = [("x", o) for o in range(1, size_x)] if size_z > 1 else []
+    for axis, offset in third_round:
+        greet(rounds.at[2], along(axis, offset))
+    send_passes(range(3, groups - 2))
+
+    def do_colour(target):
         for r in range(piece):
             y = target * piece + r
             total = zero
@@ -291,9 +307,28 @@
         def _():
             block_copy(send_colour, got_colour, 1, target).start()
 
-        return carry
-
-    lax.fori_loop(0, groups, do_colour, 0)
+    def colour_pair(pair, carry):
+        for kind, arrives in enumerate((has_before, has_after)):
+
+            @pl.when(arrives)
+            def _(kind=kind):
+                rows_copy(2 * piece, layer_recv.at[kind, pair]).wait()
+
+        @pl.when((pair == groups // 2 - 1) & has_down)
+        def _():
+            row_copy(True).wait_recv()
+
+        @pl.when((pair == groups // 2 - 1) & has_up)
+        def _():
+            row_copy(False).wait_recv()
+
+        def step(half, carry):
+            do_colour(block_at(me, pair * 2 + half))
+            return carry
+
+        return lax.fori_loop(0, 2, step, carry)
+
+    lax.fori_loop(0, groups // 2, colour_pair, 0)
 
     for r in range(piece):
         got_pass[me, r] = send_pass[me * piece + r]
@@ -336,7 +371,7 @@
     local = jnp.sum(logs, axis=0, keepdims=True)
 
     def in_first(index):
-        return {"depth": index // 2, "tile": chip * 2 + lax.rem(index, 2)}
+        return {"depth": index >> 1, "tile": chip * 2 + (index & 1)}
 
     def in_second(index):
         return {"depth": me, "tile": index * 2 + core}
@@ -351,7 +386,7 @@
                 dst_ref=parts.at[mine],
                 send_sem=sum_send.at[stage],
                 recv_sem=sum_recv.at[stage],
-                device_id=device(lax.rem(mine + offset, count)),
+                device_id=device((mine + offset) & (count - 1)),
                 device_id_type=MESH,
             ).start()
         all_but_one(parts, sum_recv.at[stage]).wait()
@@ -370,7 +405,7 @@
 
         @pl.when(sends[kind])
         def _(kind=kind):
-            halo(kind).wait_send()
+            rows_copy(rows if kind < 2 else depth_size, halo_send.at[kind]).wait()
 
     all_but_one(got_pass, block_send.at[0]).wait()
     all_but_one(got_colour, block_send.at[1]).wait()
@@ -405,7 +440,8 @@
             pltpu.SMEM((groups,), jnp.int32),
             pltpu.SemaphoreType.DMA((4,)),
             pltpu.SemaphoreType.DMA((4,)),
-            pltpu.SemaphoreType.DMA((4,)),
+            pltpu.SemaphoreType.DMA((2, groups // 2)),
+            pltpu.SemaphoreType.DMA((2,)),
             pltpu.SemaphoreType.DMA((2,)),
             pltpu.SemaphoreType.DMA((2,)),
             pltpu.SemaphoreType.DMA((2,)),

time: 35.3 us -> 35.1 us (level)
  no operation moved by 1% of the time
where the time goes in v4:
time: 35.1 us; the launch traced here: 35 us
  Pallas kernels  34.3 us (98%)
  local copies, waits for them, and re-layouts  0.62 us (2%)
    pallas_call x1, Pallas kernels, body(): pl.pallas_call(functools.partial(kernel, (groups, strips, depth_size, row...  34.3 us

profile of v4, /device:TPU:1, one launch (start us, length us, event | category | flops | bytes accessed | tf_op | source)
XLA Modules:
  0.0 35.0 jit_solution(13687239864847373203)
XLA Ops:
  0.0 34.3 %render.1 = f32[4,8,2,128]{3,2,1,0:T(2,128)S(1)} custom-call(s32[8,16,1024]{2,1,0:T(8,128)} %labels_hbm.1, s32[1,8]{1,0:T(1,128)} %order_hbm.1, s32[256]{0:T(256)} %opacity_hbm.1, s32[3,256]{1,0:T(4,128)} %colour_hbm.1), custom_call_target="tpu_custom_call" | custom-call | tf_op jit(solution)/shard_map/render/pallas_call | solution.py:422
  34.4 0.6 %copy.6 = f32[4,1,2,1024]{3,2,1,0:T(2,128)} copy(f32[4,1,2,1024]{3,2,1,0:T(2,128)S(1)} %bitcast.3) | data formatting | bytes 65536

commit v5 on v4

--- a/solution.py
+++ b/solution.py
@@ -87,19 +87,39 @@
     has_down = tile > 0
     has_after = me < groups - 1
     has_before = me > 0
-    other_core = {"depth": me, "tile": tile + 1 - 2 * core}
-    near = [(a, o) for a, n in lengths.items() if n > 1 for o in sorted({1, n - 1})]
+    ring = sorted(range(1, groups), key=lambda offset: -min(offset, groups - offset))
+    near = [(a, o) for a in ("x", "z") if lengths[a] > 1 for o in sorted({1, lengths[a] - 1})]
+
+    tuned = groups == 8
+
+    def told_later(source, target):
+        if not tuned:
+            return jnp.bool_(False)
+        late = ((source == 4) & (target < 3)) | ((source == 5) & (target < 4))
+        return late | ((source == 7) & (target == 3))
+
+    def tells(source, target):
+        late = ((source == 4) & (target < 3)) | ((source == 5) & (target < 4))
+        return late | ((source == 0) & (target == 3))
+
+    for offset in ring:
+
+        @pl.when(jnp.logical_not(told_later(me, (me + offset) & (groups - 1))))
+        def _(offset=offset):
+            greet(barrier, along("y", offset))
+
+    @pl.when(has_up)
+    def _():
+        greet(barrier, {"depth": me, "tile": tile + 1})
+
+    @pl.when(has_down)
+    def _():
+        greet(barrier, {"depth": me, "tile": tile - 1})
+
     for axis, offset in near:
         greet(barrier, along(axis, offset))
-    greet(barrier, other_core)
-    beside = jnp.where(core == 0, tile - 1, tile + 1)
-    has_beside = (beside >= 0) & (beside < strips)
-    beside_near = jnp.where(core == 0, at_x > 0, at_x < size_x - 1)
-    beside_far = jnp.logical_and(has_beside, jnp.logical_not(beside_near))
-
-    next_x = (at_x + 2 * core - 1) & (size_x - 1)
-    across = {"depth": me, "tile": (at_z * size_x + next_x) * 2 + 1 - core}
-    greet(barrier, across)
+    tidings = jnp.where(me < 4, 2, 0) if tuned else 0
+    greeted = len(ring) - tidings + len(near) + has_up.astype(jnp.int32) + has_down.astype(jnp.int32)
 
     for block in range(SUBLANES):
         pltpu.make_async_copy(
@@ -136,13 +156,12 @@
         dens[z + 1, y + 1] = (word & 255).astype(jnp.float32)
 
     def block_at(depth, step):
-        inner = groups - 2
-        turn = depth + groups // 2 - 1 + step
-        for _ in range(2):
-            turn = jnp.where(turn >= inner, turn - inner, turn)
-        swap = (depth < groups // 2).astype(jnp.int32)
-        last = jnp.where(step - inner == swap, 0, groups - 1)
-        return jnp.where(step < inner, turn + 1, last)
+        third = (groups - 2) // 2
+        turn = lax.rem(depth + step + 1, third)
+        middle = turn + (groups - third + 1) // 2
+        outer = jnp.where(turn < third // 2 + 1, turn + 1, turn + third + 1)
+        ends = jnp.where(step - (groups - 2) == (depth < groups // 2).astype(jnp.int32), 0, groups - 1)
+        return jnp.where(step < third, middle, jnp.where(step < 2 * third, outer, ends))
 
     def start_layer(kind):
         target = me + 1 if kind == 0 else me - 1
@@ -173,8 +192,8 @@
             device_id_type=MESH,
         )
 
-    def start_row(up, condition):
-        @pl.when(condition)
+    def start_row(up):
+        @pl.when(has_up if up else has_down)
         def _():
             row_copy(up).start()
 
@@ -183,7 +202,13 @@
     for y in range(rows):
         look_up(depth_size - 1, y)
         look_up(0, y)
-    pl.semaphore_wait(barrier, len(near) + 2)
+    pl.semaphore_wait(barrier, greeted)
+    for offset in ring if tuned else ():
+
+        @pl.when(tells(me, (me + offset) & (groups - 1)))
+        def _(offset=offset):
+            greet(rounds.at[3], along("y", offset))
+
 
     @pl.when(has_after)
     def _():
@@ -193,16 +218,13 @@
     def _():
         start_layer(1)
 
-    first_round = [(a, o) for a, o in near if lengths[a] >= 4]
-    for axis, offset in first_round:
+    for axis, offset in near:
         greet(rounds.at[0], along(axis, offset))
-    if size_z > 1:
-        greet(rounds.at[0], across)
     for z in range(1, depth_size - 1):
         look_up(z, 0)
         look_up(z, rows - 1)
-    start_row(True, (core == 0) | beside_near)
-    start_row(False, (core == 1) | beside_near)
+    start_row(True)
+    start_row(False)
 
     @pl.when(jnp.logical_not(has_before))
     def _():
@@ -248,23 +270,14 @@
             device_id_type=MESH,
         )
 
-    def send_passes(offsets):
-        for offset in offsets:
-            block_copy(send_pass, got_pass, 0, (me + offset) & (groups - 1)).start()
-
-    pl.semaphore_wait(rounds.at[0], len(first_round) + (size_z > 1))
-    second_round = [(a, o) for a, n in lengths.items() if n >= 8 for o in (2, n - 2)]
-    for axis, offset in second_round:
-        greet(rounds.at[1], along(axis, offset))
-    start_row(True, (core == 1) & beside_far)
-    start_row(False, (core == 0) & beside_far)
-    send_passes((2, groups - 2, 1, groups - 1))
-    if second_round:
-        pl.semaphore_wait(rounds.at[1], len(second_round))
-    third_round = [("x", o) for o in range(1, size_x)] if size_z > 1 else []
-    for axis, offset in third_round:
-        greet(rounds.at[2], along(axis, offset))
-    send_passes(range(3, groups - 2))
+    if tuned:
+
+        @pl.when(me < 4)
+        def _():
+            pl.semaphore_wait(rounds.at[3], 2)
+
+    for offset in ring:
+        block_copy(send_pass, got_pass, 0, (me + offset) & (groups - 1)).start()
 
     def do_colour(target):
         for r in range(piece):
@@ -341,8 +354,16 @@
             at = jnp.where(order[0, g] == rank, g, at)
         inverse[rank] = at
 
-    if third_round:
-        pl.semaphore_wait(rounds.at[2], len(third_round))
+    if near:
+        pl.semaphore_wait(rounds.at[0], len(near))
+    second_round = [("z", o) for o in (2, size_z - 2) if size_z >= 8]
+    for axis, offset in second_round:
+        greet(rounds.at[1], along(axis, offset))
+    if second_round:
+        pl.semaphore_wait(rounds.at[1], len(second_round))
+    third_round = [("x", o) for o in range(1, size_x) if size_z > 1]
+    for axis, offset in third_round:
+        greet(rounds.at[2], along(axis, offset))
 
     def all_but_one(ref, semaphore):
         part = ref.at[pl.ds(0, ref.shape[0] - 1)]
@@ -380,6 +401,8 @@
     for stage, (parts, mine, device) in enumerate(stages):
         count = parts.shape[0]
         parts[mine] = local
+        if stage == 1 and third_round:
+            pl.semaphore_wait(rounds.at[2], len(third_round))
         for offset in range(1, count):
             pltpu.make_async_remote_copy(
                 src_ref=parts.at[mine],
@@ -446,7 +469,7 @@
             pltpu.SemaphoreType.DMA((2,)),
             pltpu.SemaphoreType.DMA((2,)),
             pltpu.SemaphoreType.DMA((2,)),
-            pltpu.SemaphoreType.REGULAR((3,)),
+            pltpu.SemaphoreType.REGULAR((4,)),
         ],
         compiler_params=pltpu.CompilerParams(
             collective_id=0, has_side_effects=True, vmem_limit_bytes=32 * 1024 * 1024

time: 35.1 us -> 34.5 us (0.983)
  Pallas kernels: 34.3 us -> 33.7 us
    pallas_call x1, Pallas kernels: 34.3 us -> 33.7 us  [body(): pl.pallas_call(functools.partial(kernel, (groups, strips, depth_size, row...]
where the time goes in v5:
time: 34.5 us; the launch traced here: 34.4 us
  Pallas kernels  33.7 us (98%)
  local copies, waits for them, and re-layouts  0.62 us (2%)
    pallas_call x1, Pallas kernels, body(): pl.pallas_call(functools.partial(kernel, (groups, strips, depth_size, row...  33.7 us

profile of v5, /device:TPU:1, one launch (start us, length us, event | category | flops | bytes accessed | tf_op | source)
XLA Modules:
  0.0 34.4 jit_solution(1038342272353043489)
XLA Ops:
  0.0 33.7 %render.1 = f32[4,8,2,128]{3,2,1,0:T(2,128)S(1)} custom-call(s32[8,16,1024]{2,1,0:T(8,128)} %labels_hbm.1, s32[1,8]{1,0:T(1,128)} %order_hbm.1, s32[256]{0:T(256)} %opacity_hbm.1, s32[3,256]{1,0:T(4,128)} %colour_hbm.1), custom_call_target="tpu_custom_call" | custom-call | tf_op jit(solution)/shard_map/render/pallas_call | solution.py:445
  33.7 0.6 %copy.6 = f32[4,1,2,1024]{3,2,1,0:T(2,128)} copy(f32[4,1,2,1024]{3,2,1,0:T(2,128)S(1)} %bitcast.3) | data formatting | bytes 65536

commit v6 on v5

--- a/solution.py
+++ b/solution.py
@@ -1,4 +1,5 @@
 import functools
+import math
 
 import jax
 import jax.numpy as jnp
@@ -46,7 +47,6 @@
     got_colour,
     part_one,
     part_two,
-    inverse,
     load_sem,
     halo_send,
     layer_recv,
@@ -199,9 +199,13 @@
 
     sends = (has_after, has_before, has_up, has_down)
 
-    for y in range(rows):
-        look_up(depth_size - 1, y)
-        look_up(0, y)
+    def look_up_ends(row, carry):
+        for y in range(4):
+            look_up(depth_size - 1, row * 4 + y)
+            look_up(0, row * 4 + y)
+        return carry
+
+    lax.fori_loop(0, rows // 4, look_up_ends, 0)
     pl.semaphore_wait(barrier, greeted)
     for offset in ring if tuned else ():
 
@@ -220,9 +224,12 @@
 
     for axis, offset in near:
         greet(rounds.at[0], along(axis, offset))
-    for z in range(1, depth_size - 1):
+    def look_up_sides(z, carry):
         look_up(z, 0)
         look_up(z, rows - 1)
+        return carry
+
+    lax.fori_loop(1, depth_size - 1, look_up_sides, 0)
     start_row(True)
     start_row(False)
 
@@ -348,12 +355,6 @@
         for c in range(3):
             got_colour[me, r, c] = send_colour[me * piece + r, c]
 
-    for rank in range(groups):
-        at = 0
-        for g in range(1, groups):
-            at = jnp.where(order[0, g] == rank, g, at)
-        inverse[rank] = at
-
     if near:
         pl.semaphore_wait(rounds.at[0], len(near))
     second_round = [("z", o) for o in (2, size_z - 2) if size_z >= 8]
@@ -369,21 +370,47 @@
         part = ref.at[pl.ds(0, ref.shape[0] - 1)]
         return pltpu.make_async_copy(part, part, semaphore)
 
+    def in_first(index):
+        return {"depth": index >> 1, "tile": chip * 2 + (index & 1)}
+
+    def in_second(index):
+        return {"depth": me, "tile": index * 2 + core}
+
+    stages = []
+    for parts, mine, device in (
+        (part_one, me * 2 + core, in_first),
+        (part_two, chip, in_second),
+    ):
+        others = [jnp.where(k < mine, k, k + 1) for k in range(parts.shape[0] - 1)]
+        stages.append((parts, mine, [device(index) for index in others]))
+
     all_but_one(got_pass, block_recv.at[0]).wait()
+    ranks = [order[0, g] for g in range(groups)]
+    through = [[got_pass[g, r] for g in range(groups)] for r in range(piece)]
+    ahead = [[one] * groups for _ in range(piece)]
+    for g in range(groups):
+        for h in range(groups):
+            if h != g:
+                before = ranks[h] < ranks[g]
+                for r in range(piece):
+                    ahead[r][g] = ahead[r][g] * jnp.where(before, through[r][h], one)
+    for r in range(piece):
+        total = through[r][0]
+        for g in range(1, groups):
+            total = total * through[r][g]
+        frame_ref[3, :, r, :] = 1.0 - total
+        for g in range(groups):
+            got_pass[g, r] = ahead[r][g]
+
     all_but_one(got_colour, block_recv.at[1]).wait()
-
     composite = []
-    ahead = []
     for r in range(piece):
-        through = one
         sums = [zero, zero, zero]
-        for rank in range(groups):
-            g = inverse[rank]
+        for g in range(groups):
+            factor = got_pass[g, r]
             for c in range(3):
-                sums[c] = sums[c] + through * got_colour[g, r, c]
-            through = through * got_pass[g, r]
+                sums[c] = sums[c] + factor * got_colour[g, r, c]
         composite.append(sums)
-        ahead.append(through)
 
     logs = zero
     for r in range(piece):
@@ -391,38 +418,32 @@
         logs = logs + jnp.log(0.05 + lum)
     local = jnp.sum(logs, axis=0, keepdims=True)
 
-    def in_first(index):
-        return {"depth": index >> 1, "tile": chip * 2 + (index & 1)}
-
-    def in_second(index):
-        return {"depth": me, "tile": index * 2 + core}
-
-    stages = ((part_one, me * 2 + core, in_first), (part_two, chip, in_second))
-    for stage, (parts, mine, device) in enumerate(stages):
-        count = parts.shape[0]
+    for stage, (parts, mine, devices) in enumerate(stages):
         parts[mine] = local
         if stage == 1 and third_round:
             pl.semaphore_wait(rounds.at[2], len(third_round))
-        for offset in range(1, count):
+        for device in devices:
             pltpu.make_async_remote_copy(
                 src_ref=parts.at[mine],
                 dst_ref=parts.at[mine],
                 send_sem=sum_send.at[stage],
                 recv_sem=sum_recv.at[stage],
-                device_id=device((mine + offset) & (count - 1)),
+                device_id=device,
                 device_id_type=MESH,
             ).start()
         all_but_one(parts, sum_recv.at[stage]).wait()
-        local = jnp.sum(parts[...], axis=0)
+        terms = [parts[k] for k in range(parts.shape[0])]
+        while len(terms) > 1:
+            terms = [a + b for a, b in zip(terms[::2], terms[1::2], strict=True)]
+        local = terms[0]
     log_sum = jnp.sum(local, axis=1, keepdims=True)
-    scale = KEY_VALUE / jnp.exp(log_sum * (1.0 / (rows * strips * cols)))
+    scale = jnp.exp(math.log(KEY_VALUE) - log_sum * (1.0 / (rows * strips * cols)))
     scale = jnp.broadcast_to(scale, (SUBLANES, LANES))
 
     for r in range(piece):
         for c in range(3):
             scaled = composite[r][c] * scale
             frame_ref[c, :, r, :] = scaled / (1.0 + scaled)
-        frame_ref[3, :, r, :] = 1.0 - ahead[r]
 
     for kind in range(4):
 
@@ -460,7 +481,6 @@
             pltpu.VMEM((groups, piece, 3) + block, jnp.float32),
             pltpu.VMEM((groups * 2, 1, LANES), jnp.float32),
             pltpu.VMEM((strips // 2, 1, LANES), jnp.float32),
-            pltpu.SMEM((groups,), jnp.int32),
             pltpu.SemaphoreType.DMA((4,)),
             pltpu.SemaphoreType.DMA((4,)),
             pltpu.SemaphoreType.DMA((2, groups // 2)),

time: 34.5 us -> 34.3 us (level)
  no operation moved by 1% of the time
where the time goes in v6:
time: 34.3 us; the launch traced here: 34.2 us
  Pallas kernels  33.5 us (98%)
  local copies, waits for them, and re-layouts  0.62 us (2%)
    pallas_call x1, Pallas kernels, body(): pl.pallas_call(functools.partial(kernel, (groups, strips, depth_size, row...  33.5 us

profile of v6, /device:TPU:1, one launch (start us, length us, event | category | flops | bytes accessed | tf_op | source)
XLA Modules:
  0.0 34.2 jit_solution(3920841972978585066)
XLA Ops:
  0.0 33.5 %render.1 = f32[4,8,2,128]{3,2,1,0:T(2,128)S(1)} custom-call(s32[8,16,1024]{2,1,0:T(8,128)} %labels_hbm.1, s32[1,8]{1,0:T(1,128)} %order_hbm.1, s32[256]{0:T(256)} %opacity_hbm.1, s32[3,256]{1,0:T(4,128)} %colour_hbm.1), custom_call_target="tpu_custom_call" | custom-call | tf_op jit(solution)/shard_map/render/pallas_call | solution.py:466
  33.5 0.6 %copy.6 = f32[4,1,2,1024]{3,2,1,0:T(2,128)} copy(f32[4,1,2,1024]{3,2,1,0:T(2,128)S(1)} %bitcast.3) | data formatting | bytes 65536

commit v7 on v6

--- a/solution.py
+++ b/solution.py
@@ -116,9 +116,27 @@
     def _():
         greet(barrier, {"depth": me, "tile": tile - 1})
 
-    for axis, offset in near:
-        greet(barrier, along(axis, offset))
+    halves = size_z == 8
+    late_z = {1: at_z == 7, 7: at_z == 4} if halves else {}
+    first_z = (at_z == 0) | (at_z == 3)
+    early_z = {1: first_z, 7: first_z} if halves else {}
+
+    def greet_near(semaphore, but, only=False):
+        for axis, offset in near:
+            special = but.get(offset) if axis == "z" else None
+            if special is None:
+                if not only:
+                    greet(semaphore, along(axis, offset))
+                continue
+
+            @pl.when(special if only else jnp.logical_not(special))
+            def _(axis=axis, offset=offset):
+                greet(semaphore, along(axis, offset))
+
+    greet_near(barrier, late_z)
     tidings = jnp.where(me < 4, 2, 0) if tuned else 0
+    if halves:
+        tidings = tidings + first_z.astype(jnp.int32)
     greeted = len(ring) - tidings + len(near) + has_up.astype(jnp.int32) + has_down.astype(jnp.int32)
 
     for block in range(SUBLANES):
@@ -158,10 +176,12 @@
     def block_at(depth, step):
         third = (groups - 2) // 2
         turn = lax.rem(depth + step + 1, third)
-        middle = turn + (groups - third + 1) // 2
-        outer = jnp.where(turn < third // 2 + 1, turn + 1, turn + third + 1)
-        ends = jnp.where(step - (groups - 2) == (depth < groups // 2).astype(jnp.int32), 0, groups - 1)
-        return jnp.where(step < third, middle, jnp.where(step < 2 * third, outer, ends))
+        flip = (depth + step) & 1
+        return jnp.where(
+            step < third,
+            turn + 4,
+            jnp.where(step < 5, jnp.where(flip == 0, 3, 7), jnp.where(step < 7, 2 - flip, 0)),
+        )
 
     def start_layer(kind):
         target = me + 1 if kind == 0 else me - 1
@@ -222,8 +242,7 @@
     def _():
         start_layer(1)
 
-    for axis, offset in near:
-        greet(rounds.at[0], along(axis, offset))
+    greet_near(rounds.at[0], early_z)
     def look_up_sides(z, carry):
         look_up(z, 0)
         look_up(z, rows - 1)
@@ -334,11 +353,11 @@
             def _(kind=kind):
                 rows_copy(2 * piece, layer_recv.at[kind, pair]).wait()
 
-        @pl.when((pair == groups // 2 - 1) & has_down)
+        @pl.when((pair == 1) & has_down)
         def _():
             row_copy(True).wait_recv()
 
-        @pl.when((pair == groups // 2 - 1) & has_up)
+        @pl.when((pair == 1) & has_up)
         def _():
             row_copy(False).wait_recv()
 
@@ -357,6 +376,7 @@
 
     if near:
         pl.semaphore_wait(rounds.at[0], len(near))
+        greet_near(rounds.at[0], early_z, only=True)
     second_round = [("z", o) for o in (2, size_z - 2) if size_z >= 8]
     for axis, offset in second_round:
         greet(rounds.at[1], along(axis, offset))

time: 34.3 us -> 34.2 us (level)
  no operation moved by 1% of the time
where the time goes in v7:
time: 34.2 us; the launch traced here: 34.1 us
  Pallas kernels  33.4 us (98%)
  local copies, waits for them, and re-layouts  0.62 us (2%)
    pallas_call x1, Pallas kernels, body(): pl.pallas_call(functools.partial(kernel, (groups, strips, depth_size, row...  33.4 us

profile of v7, /device:TPU:1, one launch (start us, length us, event | category | flops | bytes accessed | tf_op | source)
XLA Modules:
  0.0 34.1 jit_solution(15106385662230335460)
XLA Ops:
  0.0 33.4 %render.1 = f32[4,8,2,128]{3,2,1,0:T(2,128)S(1)} custom-call(s32[8,16,1024]{2,1,0:T(8,128)} %labels_hbm.1, s32[1,8]{1,0:T(1,128)} %order_hbm.1, s32[256]{0:T(256)} %opacity_hbm.1, s32[3,256]{1,0:T(4,128)} %colour_hbm.1), custom_call_target="tpu_custom_call" | custom-call | tf_op jit(solution)/shard_map/render/pallas_call | solution.py:486
  33.4 0.6 %copy.6 = f32[4,1,2,1024]{3,2,1,0:T(2,128)} copy(f32[4,1,2,1024]{3,2,1,0:T(2,128)S(1)} %bitcast.3) | data formatting | bytes 65536

commit v8 on v7

--- a/solution.py
+++ b/solution.py
@@ -451,6 +451,16 @@
                 device_id=device,
                 device_id_type=MESH,
             ).start()
+        if stage == 1:
+            for kind in range(4):
+
+                @pl.when(sends[kind])
+                def _(kind=kind):
+                    rows_copy(rows if kind < 2 else depth_size, halo_send.at[kind]).wait()
+
+            all_but_one(got_pass, block_send.at[0]).wait()
+            all_but_one(got_colour, block_send.at[1]).wait()
+        all_but_one(parts, sum_send.at[stage]).wait()
         all_but_one(parts, sum_recv.at[stage]).wait()
         terms = [parts[k] for k in range(parts.shape[0])]
         while len(terms) > 1:
@@ -464,17 +474,6 @@
         for c in range(3):
             scaled = composite[r][c] * scale
             frame_ref[c, :, r, :] = scaled / (1.0 + scaled)
-
-    for kind in range(4):
-
-        @pl.when(sends[kind])
-        def _(kind=kind):
-            rows_copy(rows if kind < 2 else depth_size, halo_send.at[kind]).wait()
-
-    all_but_one(got_pass, block_send.at[0]).wait()
-    all_but_one(got_colour, block_send.at[1]).wait()
-    all_but_one(part_one, sum_send.at[0]).wait()
-    all_but_one(part_two, sum_send.at[1]).wait()
 
 
 def body(labels, depth_order, opacity_table, colour_map):

time: 34.2 us -> 34.2 us (level)
  no operation moved by 1% of the time
where the time goes in v8:
time: 34.2 us; the launch traced here: 34 us
  Pallas kernels  33.4 us (98%)
  local copies, waits for them, and re-layouts  0.62 us (2%)
    pallas_call x1, Pallas kernels, body(): pl.pallas_call(functools.partial(kernel, (groups, strips, depth_size, row...  33.4 us

profile of v8, /device:TPU:1, one launch (start us, length us, event | category | flops | bytes accessed | tf_op | source)
XLA Modules:
  0.0 34.0 jit_solution(10935907359003742197)
XLA Ops:
  0.0 33.4 %render.1 = f32[4,8,2,128]{3,2,1,0:T(2,128)S(1)} custom-call(s32[8,16,1024]{2,1,0:T(8,128)} %labels_hbm.1, s32[1,8]{1,0:T(1,128)} %order_hbm.1, s32[256]{0:T(256)} %opacity_hbm.1, s32[3,256]{1,0:T(4,128)} %colour_hbm.1), custom_call_target="tpu_custom_call" | custom-call | tf_op jit(solution)/shard_map/render/pallas_call | solution.py:485
  33.4 0.6 %copy.6 = f32[4,1,2,1024]{3,2,1,0:T(2,128)} copy(f32[4,1,2,1024]{3,2,1,0:T(2,128)S(1)} %bitcast.3) | data formatting | bytes 65536
